TPU v7x, 32 devices: a whole 2x2x4 slice. The times are simulated.
32 devices in a mesh: box: 8 (over z, core), sub: 4 (over y, x).
Axes of the slice: x: 2, y: 2, z: 4, core: 2. Of those that a mesh axis runs over, the one named last changes fastest.
Arguments:
- right_side: float32 [64, 128, 256], P('box', 'sub'), may hold values from -6 to 6
- beta: float32 [64, 128, 256], P('box', 'sub'), may hold values from 0.2 to 5
Outputs:
- pressure: float32 [64, 128, 256], P('box', 'sub')
- residual: float32 [64, 128, 256], P('box', 'sub')
All inputs are finite; a program needn't handle non-finite values.
Results may differ from a plain program's by a relative error of at most 0.0003.
Values sent between devices are 32-bit elements; how exact they have to be, the bound alone decides.
A program may use at most 192 MiB of HBM per device.

v0:
```python
import jax
import jax.numpy as jnp
from jax import lax
from jax.sharding import PartitionSpec as P

ITERS = 8


def with_halo(value, sides, width):
    for axis, dim in sides:
        size, length = (lax.axis_size(axis), value.shape[dim])
        up = [(i, (i + 1) % size) for i in range(size - 1)]
        down = [(j, i) for i, j in up]
        last = lax.slice_in_dim(value, length - width, length, axis=dim)
        first = lax.slice_in_dim(value, 0, width, axis=dim)
        before = lax.ppermute(last, axis, up)
        after = lax.ppermute(first, axis, down)
        value = jnp.concatenate([before, value, after], axis=dim)
    return value


def sides(padded):
    return (
        padded[:-2, 1:-1, 1:-1],
        padded[2:, 1:-1, 1:-1],
        padded[1:-1, :-2, 1:-1],
        padded[1:-1, 2:, 1:-1],
        padded[1:-1, 1:-1, :-2],
        padded[1:-1, 1:-1, 2:],
    )


def coefficients(beta_pad):
    center = beta_pad[1:-1, 1:-1, 1:-1]
    faces = jnp.stack([0.5 * (center + side) for side in sides(beta_pad)])
    return (faces, jnp.sum(faces, axis=0))


def neighbour_sum(padded, faces):
    total = jnp.zeros(faces.shape[1:], faces.dtype)
    for index, side in enumerate(sides(padded)):
        total = total + faces[index] * side
    return total


def face_cells(field):
    grown = with_halo(field, (("box", 0), ("sub", 1)), 1)
    return jnp.pad(grown, ((0, 0), (0, 0), (1, 1)))


def red_cells(shape):
    parity = (
        lax.broadcasted_iota(jnp.int32, shape, 0)
        + lax.broadcasted_iota(jnp.int32, shape, 1)
        + lax.broadcasted_iota(jnp.int32, shape, 2)
    ) % 2
    return parity == 0


def relax(field, source, faces, diag, mask):
    return jnp.where(mask, (source + neighbour_sum(face_cells(field), faces)) / diag, field)


def first_sweep(source, faces, diag):
    red = red_cells(source.shape)
    field = jnp.where(red, source / diag, 0.0)
    return relax(field, source, faces, diag, jnp.logical_not(red))


def sweep(field, source, faces, diag):
    red = red_cells(field.shape)
    field = relax(field, source, faces, diag, red)
    return relax(field, source, faces, diag, jnp.logical_not(red))


def remainder(field, source, faces, diag):
    return source - (diag * field - neighbour_sum(face_cells(field), faces))


def restrict(field, factor):
    nx, ny, nz = field.shape
    return field.reshape(nx // 2, 2, ny // 2, 2, nz // 2, 2).sum(axis=(1, 3, 5)) * factor


def prolong(field):
    return jnp.repeat(jnp.repeat(jnp.repeat(field, 2, 0), 2, 1), 2, 2)


def solve_plain(source, faces, diag, grow, curv_total, norm_total):
    solved = jnp.zeros_like(source)
    resid = source
    precond = resid / diag
    direction = precond
    rz_now = norm_total(jnp.sum(resid * precond))
    for step in range(ITERS):
        image = diag * direction - neighbour_sum(grow(direction), faces)
        alpha = rz_now / curv_total(jnp.sum(direction * image))
        solved = solved + alpha * direction
        resid = resid - alpha * image
        if step + 1 < ITERS:
            precond = resid / diag
            rz_next = norm_total(jnp.sum(resid * precond))
            direction = precond + rz_next / rz_now * direction
            rz_now = rz_next
    return solved


def shards(right_side, beta):
    faces_f, diag_f = coefficients(face_cells(beta))
    pressure_pre = first_sweep(right_side, faces_f, diag_f)
    fine_resid = remainder(pressure_pre, right_side, faces_f, diag_f)
    medium_beta = restrict(beta, 0.125)
    medium_rhs = restrict(fine_resid, 0.5)
    faces_m, diag_m = coefficients(face_cells(medium_beta))
    medium_pre = first_sweep(medium_rhs, faces_m, diag_m)
    medium_resid = remainder(medium_pre, medium_rhs, faces_m, diag_m)
    coarse_beta = restrict(medium_beta, 0.125)
    coarse_rhs = restrict(medium_resid, 0.5)

    def grow(field):
        grown = with_halo(field, (("box", 0), ("sub", 1)), 1)
        return jnp.pad(grown, ((0, 0), (0, 0), (1, 1)))

    def curv_total(value):
        return lax.psum(value, ("box", "sub"))

    def norm_total(value):
        return lax.psum(value, ("box", "sub"))

    source_c, beta_c = (coarse_rhs, coarse_beta)
    faces_c, diag_c = coefficients(grow(beta_c))
    solved = solve_plain(source_c, faces_c, diag_c, grow, curv_total, norm_total)
    medium_post = sweep(medium_pre + prolong(solved), medium_rhs, faces_m, diag_m)
    pressure = sweep(pressure_pre + prolong(medium_post), right_side, faces_f, diag_f)
    residual = remainder(pressure, right_side, faces_f, diag_f)
    return (pressure, residual)


def solution(mesh):
    placed = (P("box", "sub", None), P("box", "sub", None))
    return jax.shard_map(
        shards,
        mesh=mesh,
        in_specs=placed,
        out_specs=(P("box", "sub", None), P("box", "sub", None)),
        check_vma=False,
    )
```

profile of v0, /device:TPU:0, one launch (start us, length us, event | category | flops | bytes accessed | tf_op | source)
XLA Modules:
  0.0 1011.4 jit_solution(3898526116363727308)
XLA Ops:
  10.4 4.7 collective-permute-start.2
  15.1 18.8 %reshape.72 = f32[4,2,16,2,128,2]{5,4,3,2,1,0:T(8,128)} reshape(f32[8,32,256]{2,1,0:T(8,128)} %param.3) | data formatting | bytes 524288 | tf_op jit(solution)/shard_map/reshape | solution.py:82
  33.9 7.0 reduce_sum.243
  48.8 4.3 collective-permute-start.6
  55.7 4.9 collective-permute-start.12
  72.9 4.9 collective-permute-start.14
  77.8 4.8 collective-permute-start.10
  88.8 18.1 %reshape.71 = f32[4,2,16,2,128,2]{5,4,3,2,1,0:T(8,128)} reshape(f32[8,32,256]{2,1,0:T(8,128)S(1)} %fusion.40) | data formatting | bytes 524288 | tf_op jit(solution)/shard_map/reshape | solution.py:82
  106.9 7.0 reduce_sum.242
  116.6 4.2 collective-permute-done.17
  136.8 5.0 collective-permute-start.26
  141.9 4.8 collective-permute-start.22
  161.4 5.0 collective-permute-done.29
  175.4 40.5 %all-reduce.20 = (f32[]{:T(128)}, f32[]{:T(128)}) all-reduce(f32[]{:T(128)} %get-tuple-element.11, f32[]{:T(128)} %get-tuple-element.10), channel_id=1, replica_groups=mesh['box'=8,'sub'=4] {'box','sub'}, use_global_device_ids=true, to_apply=%region_5.6 | all-reduce | flops 2 | bytes 16 | tf_op jit(solution)/shard_map/psum | solution.py:128
  217.9 40.8 %psum.114 = f32[]{:T(128)} all-reduce(f32[]{:T(128)} %get-tuple-element.41), channel_id=1, replica_groups=mesh['box'=8,'sub'=4] {'box','sub'}, use_global_device_ids=true, to_apply=%region_9.10 | all-reduce | flops 1 | bytes 8 | tf_op jit(solution)/shard_map/psum | solution.py:128
  275.6 40.9 %psum.115 = f32[]{:T(128)} all-reduce(f32[]{:T(128)} %get-tuple-element.39), channel_id=1, replica_groups=mesh['box'=8,'sub'=4] {'box','sub'}, use_global_device_ids=true, to_apply=%region_11.12 | all-reduce | flops 1 | bytes 8 | tf_op jit(solution)/shard_map/psum | solution.py:125
  318.5 41.6 %psum.116 = f32[]{:T(128)} all-reduce(f32[]{:T(128)} %get-tuple-element.36), channel_id=1, replica_groups=mesh['box'=8,'sub'=4] {'box','sub'}, use_global_device_ids=true, to_apply=%region_13.14 | all-reduce | flops 1 | bytes 8 | tf_op jit(solution)/shard_map/psum | solution.py:128
  377.1 41.0 %psum.117 = f32[]{:T(128)} all-reduce(f32[]{:T(128)} %get-tuple-element.34), channel_id=1, replica_groups=mesh['box'=8,'sub'=4] {'box','sub'}, use_global_device_ids=true, to_apply=%region_15.16 | all-reduce | flops 1 | bytes 8 | tf_op jit(solution)/shard_map/psum | solution.py:125
  420.1 41.5 %psum.118 = f32[]{:T(128)} all-reduce(f32[]{:T(128)} %get-tuple-element.31), channel_id=1, replica_groups=mesh['box'=8,'sub'=4] {'box','sub'}, use_global_device_ids=true, to_apply=%region_17.18 | all-reduce | flops 1 | bytes 8 | tf_op jit(solution)/shard_map/psum | solution.py:128
  478.6 41.0 %psum.119 = f32[]{:T(128)} all-reduce(f32[]{:T(128)} %get-tuple-element.29), channel_id=1, replica_groups=mesh['box'=8,'sub'=4] {'box','sub'}, use_global_device_ids=true, to_apply=%region_19.20 | all-reduce | flops 1 | bytes 8 | tf_op jit(solution)/shard_map/psum | solution.py:125
  521.6 41.5 %psum.120 = f32[]{:T(128)} all-reduce(f32[]{:T(128)} %get-tuple-element.26), channel_id=1, replica_groups=mesh['box'=8,'sub'=4] {'box','sub'}, use_global_device_ids=true, to_apply=%region_21.22 | all-reduce | flops 1 | bytes 8 | tf_op jit(solution)/shard_map/psum | solution.py:128
  580.1 41.0 %psum.121 = f32[]{:T(128)} all-reduce(f32[]{:T(128)} %get-tuple-element.24), channel_id=1, replica_groups=mesh['box'=8,'sub'=4] {'box','sub'}, use_global_device_ids=true, to_apply=%region_23.24 | all-reduce | flops 1 | bytes 8 | tf_op jit(solution)/shard_map/psum | solution.py:125
  623.0 41.5 %psum.122 = f32[]{:T(128)} all-reduce(f32[]{:T(128)} %get-tuple-element.21), channel_id=1, replica_groups=mesh['box'=8,'sub'=4] {'box','sub'}, use_global_device_ids=true, to_apply=%region_25.26 | all-reduce | flops 1 | bytes 8 | tf_op jit(solution)/shard_map/psum | solution.py:128
  681.5 40.9 %psum.123 = f32[]{:T(128)} all-reduce(f32[]{:T(128)} %get-tuple-element.19), channel_id=1, replica_groups=mesh['box'=8,'sub'=4] {'box','sub'}, use_global_device_ids=true, to_apply=%region_27.28 | all-reduce | flops 1 | bytes 8 | tf_op jit(solution)/shard_map/psum | solution.py:125
  724.4 41.8 %psum.124 = f32[]{:T(128)} all-reduce(f32[]{:T(128)} %get-tuple-element.16), channel_id=1, replica_groups=mesh['box'=8,'sub'=4] {'box','sub'}, use_global_device_ids=true, to_apply=%region_29.30 | all-reduce | flops 1 | bytes 8 | tf_op jit(solution)/shard_map/psum | solution.py:128
  783.2 40.8 %psum.125 = f32[]{:T(128)} all-reduce(f32[]{:T(128)} %get-tuple-element.14), channel_id=1, replica_groups=mesh['box'=8,'sub'=4] {'box','sub'}, use_global_device_ids=true, to_apply=%region_31.32 | all-reduce | flops 1 | bytes 8 | tf_op jit(solution)/shard_map/psum | solution.py:125
  826.0 41.7 %psum.126 = f32[]{:T(128)} all-reduce(f32[]{:T(128)} %multiply_reduce_fusion), channel_id=1, replica_groups=mesh['box'=8,'sub'=4] {'box','sub'}, use_global_device_ids=true, to_apply=%region_33.34 | all-reduce | flops 1 | bytes 8 | tf_op jit(solution)/shard_map/psum | solution.py:128
  884.7 40.8 %psum.127 = f32[]{:T(128)} all-reduce(f32[]{:T(128)} %fusion.135), channel_id=1, replica_groups=mesh['box'=8,'sub'=4] {'box','sub'}, use_global_device_ids=true, to_apply=%region_35.36 | all-reduce | flops 1 | bytes 8 | tf_op jit(solution)/shard_map/psum | solution.py:125
  950.0 4.5 collective-permute-start.66
  973.3 4.2 collective-permute-done.71
  989.6 4.2 collective-permute-done.75
  1005.9 4.2 collective-permute-done.79
  (270 shorter events, 261.1 us)
Async XLA Ops:
  9.1 31.8 %collective-permute-start.3 = (f32[10,1,256]{2,1,0:T(1,128)S(1)}, f32[10,1,256]{2,1,0:T(1,128)S(1)}, u32[]{:S(2)}, u32[]{:S(2)}) collective-permute-start(f32[10,1,256]{2,1,0:T(1,128)S(1)} %get-tuple-element.73), channel_id=1, source_target_pairs={{1,0},{2,1},{3,2},{5,4},{6,5},{7,6},{9,8},{10,9},{11,10},{13,12},{... | collective-permute-start | bytes 30728 | tf_op jit(solution)/shard_map/ppermute | solution.py:17
  10.4 30.5 %collective-permute-start.2 = (f32[10,1,256]{2,1,0:T(1,128)S(1)}, f32[10,1,256]{2,1,0:T(1,128)S(1)}, u32[]{:S(2)}, u32[]{:S(2)}) collective-permute-start(f32[10,1,256]{2,1,0:T(1,128)S(1)} %get-tuple-element.74), channel_id=1, source_target_pairs={{0,1},{1,2},{2,3},{4,5},{5,6},{6,7},{8,9},{9,10},{10,11},{12,13},{... | collective-permute-start | bytes 30728 | tf_op jit(solution)/shard_map/ppermute | solution.py:16
  48.8 17.1 %collective-permute-start.6 = (f32[10,1,256]{2,1,0:T(1,128)S(1)}, f32[10,1,256]{2,1,0:T(1,128)S(1)}, u32[]{:S(2)}, u32[]{:S(2)}) collective-permute-start(f32[10,1,256]{2,1,0:T(1,128)S(1)} %get-tuple-element.71), channel_id=1, source_target_pairs={{0,1},{1,2},{2,3},{4,5},{5,6},{6,7},{8,9},{9,10},{10,11},{12,13},{... | collective-permute-start | bytes 30728 | tf_op jit(solution)/shard_map/ppermute | solution.py:16
  53.1 12.8 %collective-permute-start.7 = (f32[10,1,256]{2,1,0:T(1,128)S(1)}, f32[10,1,256]{2,1,0:T(1,128)S(1)}, u32[]{:S(2)}, u32[]{:S(2)}) collective-permute-start(f32[10,1,256]{2,1,0:T(1,128)S(1)} %get-tuple-element.72), channel_id=1, source_target_pairs={{1,0},{2,1},{3,2},{5,4},{6,5},{7,6},{9,8},{10,9},{11,10},{13,12},{... | collective-permute-start | bytes 30728 | tf_op jit(solution)/shard_map/ppermute | solution.py:17
  54.4 17.1 %collective-permute-start.13 = (f32[1,16,128]{2,1,0:T(8,128)S(1)}, f32[1,16,128]{2,1,0:T(8,128)S(1)}, u32[]{:S(2)}, u32[]{:S(2)}) collective-permute-start(f32[1,16,128]{2,1,0:T(8,128)S(1)} %get-tuple-element.105), channel_id=1, source_target_pairs={{4,0},{8,4},{12,8},{16,12},{20,16},{24,20},{28,24},{5,1},{9,5},{13... | collective-permute-start | bytes 24584 | tf_op jit(solution)/shard_map/ppermute | solution.py:17
  55.7 15.8 %collective-permute-start.12 = (f32[1,16,128]{2,1,0:T(8,128)S(1)}, f32[1,16,128]{2,1,0:T(8,128)S(1)}, u32[]{:S(2)}, u32[]{:S(2)}) collective-permute-start(f32[1,16,128]{2,1,0:T(8,128)S(1)} %get-tuple-element.106), channel_id=1, source_target_pairs={{0,4},{4,8},{8,12},{12,16},{16,20},{20,24},{24,28},{1,5},{5,9},{9,... | collective-permute-start | bytes 24584 | tf_op jit(solution)/shard_map/ppermute | solution.py:16
  66.6 11.2 %collective-permute-start.8 = (f32[1,32,256]{2,1,0:T(8,128)S(1)}, f32[1,32,256]{2,1,0:T(8,128)S(1)}, u32[]{:S(2)}, u32[]{:S(2)}) collective-permute-start(f32[1,32,256]{2,1,0:T(8,128)S(1)} %get-tuple-element.81), channel_id=1, source_target_pairs={{0,4},{4,8},{8,12},{12,16},{16,20},{20,24},{24,28},{1,5},{5,9},{9,... | collective-permute-start | bytes 98312 | tf_op jit(solution)/shard_map/ppermute | solution.py:16
  70.2 7.6 collective-permute-start.9
  71.6 12.4 %collective-permute-start.15 = (f32[6,1,128]{2,1,0:T(1,128)S(1)}, f32[6,1,128]{2,1,0:T(1,128)S(1)}, u32[]{:S(2)}, u32[]{:S(2)}) collective-permute-start(f32[6,1,128]{2,1,0:T(1,128)S(1)} %get-tuple-element.95), channel_id=1, source_target_pairs={{1,0},{2,1},{3,2},{5,4},{6,5},{7,6},{9,8},{10,9},{11,10},{13,12},{... | collective-permute-start | bytes 9224 | tf_op jit(solution)/shard_map/ppermute | solution.py:17
  72.9 11.1 %collective-permute-start.14 = (f32[6,1,128]{2,1,0:T(1,128)S(1)}, f32[6,1,128]{2,1,0:T(1,128)S(1)}, u32[]{:S(2)}, u32[]{:S(2)}) collective-permute-start(f32[6,1,128]{2,1,0:T(1,128)S(1)} %get-tuple-element.96), channel_id=1, source_target_pairs={{0,1},{1,2},{2,3},{4,5},{5,6},{6,7},{8,9},{9,10},{10,11},{12,13},{... | collective-permute-start | bytes 9224 | tf_op jit(solution)/shard_map/ppermute | solution.py:16
  77.8 6.3 collective-permute-start.10
  82.6 5.6 collective-permute-start.11
  115.3 5.6 collective-permute-start.17
  120.9 10.0 collective-permute-start.18
  124.3 6.7 collective-permute-start.19
  125.6 9.9 collective-permute-start.24
  129.6 5.9 collective-permute-start.25
  131.2 10.7 %collective-permute-start.20 = (f32[1,16,128]{2,1,0:T(8,128)S(1)}, f32[1,16,128]{2,1,0:T(8,128)S(1)}, u32[]{:S(2)}, u32[]{:S(2)}) collective-permute-start(f32[1,16,128]{2,1,0:T(8,128)S(1)} %get-tuple-element.101), channel_id=1, source_target_pairs={{0,4},{4,8},{8,12},{12,16},{16,20},{20,24},{24,28},{1,5},{5,9},{9,... | collective-permute-start | bytes 24584 | tf_op jit(solution)/shard_map/ppermute | solution.py:16
  134.2 7.7 collective-permute-start.21
  135.5 12.7 %collective-permute-start.27 = (f32[4,1,64]{2,1,0:T(1,128)S(1)}, f32[4,1,64]{2,1,0:T(1,128)S(1)}, u32[]{:S(2)}, u32[]{:S(2)}) collective-permute-start(f32[4,1,64]{2,1,0:T(1,128)S(1)} %get-tuple-element.123), channel_id=1, source_target_pairs={{1,0},{2,1},{3,2},{5,4},{6,5},{7,6},{9,8},{10,9},{11,10},{13,12},{... | collective-permute-start | bytes 3080 | tf_op jit(solution)/shard_map/ppermute | solution.py:17
  136.8 11.4 %collective-permute-start.26 = (f32[4,1,64]{2,1,0:T(1,128)S(1)}, f32[4,1,64]{2,1,0:T(1,128)S(1)}, u32[]{:S(2)}, u32[]{:S(2)}) collective-permute-start(f32[4,1,64]{2,1,0:T(1,128)S(1)} %get-tuple-element.124), channel_id=1, source_target_pairs={{0,1},{1,2},{2,3},{4,5},{5,6},{6,7},{8,9},{9,10},{10,11},{12,13},{... | collective-permute-start | bytes 3080 | tf_op jit(solution)/shard_map/ppermute | solution.py:16
  141.9 6.4 collective-permute-start.22
  146.7 5.5 collective-permute-start.23
  160.1 6.3 collective-permute-start.29
  265.2 5.5 collective-permute-start.34
  366.7 5.5 collective-permute-start.38
  937.3 5.5 collective-permute-start.63
  950.0 5.8 collective-permute-start.66
  954.5 5.5 collective-permute-start.67
  971.9 5.6 collective-permute-start.71
  988.2 5.6 collective-permute-start.75
  1004.5 5.6 collective-permute-start.79
  (51 other events, 282.9 us)
where the time goes:
time: 1020 us; the launch traced here: 1010 us
  blocking collectives  617 us (60%)
  starting transfers between devices  182 us (18%)
  waiting for transfers between devices  109 us (11%)
  local copies, waits for them, and re-layouts  46.7 us (5%)
  other arithmetic  34.2 us (3%)
  between operations  22.3 us (2%)
    psum x8, blocking collectives, norm_total(): return lax.psum(value, ('box', 'sub'))  331 us
    psum x7, blocking collectives, curv_total(): return lax.psum(value, ('box', 'sub'))  287 us
    ppermute x40, starting transfers between devices, with_halo(): before = lax.ppermute(last, axis, up)  130 us
    ppermute x40, waiting for transfers between devices, with_halo(): after = lax.ppermute(first, axis, down)  109 us
    ppermute x40, starting transfers between devices, with_halo(): after = lax.ppermute(first, axis, down)  51.9 us
    reshape x3, local copies, waits for them, and re-layouts, restrict(): field.reshape(nx // 2, 2, ny // 2, 2, nz // 2, 2).sum(axis=(1, 3, 5))  40.3 us
  transfers between devices with their start and end apart: 80, of which 34 were waited for; matrix products, arithmetic and copies ran while one was open for 3% of the time, Pallas kernels for 0%

commit v1 on v0

v1 whole, which is shorter than its diff:
```python
import functools

import jax
import jax.numpy as jnp
from jax import lax
from jax.experimental import pallas as pl
from jax.experimental.pallas import tpu as pltpu
from jax.sharding import PartitionSpec as P

ITERS = 8
HB = 5
HG = 4
HY = 8
HM = 4
DIRECTIONS = [(dx, dy) for dx in (-1, 0, 1) for dy in (-1, 0, 1) if (dx, dy) != (0, 0)]
HIGHEST = lax.Precision.HIGHEST


def span(step, size, width, halo):
    if step == 0:
        return 0, halo, size
    if step > 0:
        return size - width, halo - width, width
    return 0, halo + size, width


def shifted(value, step, axis):
    return pltpu.roll(value, (-step) % value.shape[axis], axis)


def kernel(nb, ns, g_in, b_in, p_out, r_out, B, G, CX, CYP, CYM, CZP, CZM, D, I, V, TMP,
           BM, GM, MX, MYP, MYM, MZP, MZM, DM, IM, W, PM, CB, CR, XC, CXP, CXM, KYP, KYM, KZP, KZM, DC, IC,
           RR, PP, own_sem, fine_send, fine_recv, med_send, med_recv, box_send, box_recv, sub_send, sub_recv):
    nx, ny, nz = g_in.shape
    mx, my, mz = nx // 2, ny // 2, nz // 2
    cy = my // 2
    rows, mrows = ny + 2 * HY, my + 2 * HY
    box, sub = lax.axis_index("box"), lax.axis_index("sub")

    def exists(dx, dy):
        ok = None
        for step, at, size in ((dx, box, nb), (dy, sub, ns)):
            here = None if step == 0 else (at + step < size if step > 0 else at + step >= 0)
            ok = here if ok is None else (ok if here is None else jnp.logical_and(ok, here))
        return ok

    def halo(src, dst, own, width_x, halo_x, sends, recvs, from_ext):
        out = []
        for k, (dx, dy) in enumerate(DIRECTIONS):
            sx, tx, lx = span(dx, own[0], width_x, halo_x)
            sy, ty, ly = span(dy, own[1], HY, HY)
            if from_ext:
                sx, sy = sx + halo_x, sy + HY
            out.append(pltpu.make_async_remote_copy(
                src_ref=src.at[pl.ds(sx, lx), pl.ds(sy, ly), :],
                dst_ref=dst.at[pl.ds(tx, lx), pl.ds(ty, ly), :],
                send_sem=sends.at[k], recv_sem=recvs.at[k],
                device_id={"box": box + dx, "sub": sub + dy},
                device_id_type=pl.DeviceIdType.MESH))
        return out

    def start(copies):
        for (dx, dy), copy in zip(DIRECTIONS, copies):
            pl.when(exists(dx, dy))(copy.start)

    def wait_recv(copies):
        for (dx, dy), copy in zip(DIRECTIONS, copies):
            pl.when(exists(-dx, -dy))(copy.wait_recv)

    def wait_send(copies):
        for (dx, dy), copy in zip(DIRECTIONS, copies):
            pl.when(exists(dx, dy))(copy.wait_send)

    def clear(dst, own, width_x, halo_x):
        for dx, dy in DIRECTIONS:
            _, tx, lx = span(dx, own[0], width_x, halo_x)
            _, ty, ly = span(dy, own[1], HY, HY)

            @pl.when(jnp.logical_not(exists(-dx, -dy)))
            def _():
                dst[pl.ds(tx, lx), pl.ds(ty, ly), :] = jnp.zeros((lx, ly, dst.shape[2]), jnp.float32)

    beta_halo = halo(b_in, B, (nx, ny), HB, HB, fine_send.at[0], fine_recv.at[0], False)
    rhs_halo = halo(g_in, G, (nx, ny), HG, HB, fine_send.at[1], fine_recv.at[1], False)
    own_b = pltpu.make_async_copy(b_in, B.at[pl.ds(HB, nx), pl.ds(HY, ny), :], own_sem.at[0])
    own_g = pltpu.make_async_copy(g_in, G.at[pl.ds(HB, nx), pl.ds(HY, ny), :], own_sem.at[1])
    own_b.start()
    start(beta_halo)
    start(rhs_halo)
    own_g.start()

    pair_sum = (lax.broadcasted_iota(jnp.int32, (nz, mz), 0) >> 1
                == lax.broadcasted_iota(jnp.int32, (nz, mz), 1)).astype(jnp.float32)
    spread = (lax.broadcasted_iota(jnp.int32, (mz, nz), 1) >> 1
              == lax.broadcasted_iota(jnp.int32, (mz, nz), 0)).astype(jnp.float32)

    def restrict(planes, factor):
        n = planes.shape[0]
        TMP[0:n, :] = jnp.dot(planes, pair_sum, precision=HIGHEST, preferred_element_type=jnp.float32)
        return (TMP[pl.ds(0, n // 2, stride=2), :] + TMP[pl.ds(1, n // 2, stride=2), :]) * factor

    def pack(planes):
        return jnp.concatenate([planes[0] + planes[1], planes[2] + planes[3]], axis=1)

    def gather(buffer, index):
        def block(b, s, size):
            return buffer.at[pl.ds(b, size), pl.ds(pl.multiple_of(s * cy, cy), cy), :]
        first = [pltpu.make_async_remote_copy(
            src_ref=block(box, sub, 1), dst_ref=block(box, sub, 1),
            send_sem=box_send.at[index, k], recv_sem=box_recv.at[index, k],
            device_id={"box": lax.rem(box + k + 1, nb), "sub": sub}, device_id_type=pl.DeviceIdType.MESH)
            for k in range(nb - 1)]
        second = [pltpu.make_async_remote_copy(
            src_ref=block(0, sub, nb), dst_ref=block(0, sub, nb),
            send_sem=sub_send.at[index, k], recv_sem=sub_recv.at[index, k],
            device_id={"box": box, "sub": lax.rem(sub + k + 1, ns)}, device_id_type=pl.DeviceIdType.MESH)
            for k in range(ns - 1)]
        return first, second

    own_b.wait()
    for k in range(mx):
        summed = B[HB + 2 * k, pl.ds(HY, ny), :] + B[HB + 2 * k + 1, pl.ds(HY, ny), :]
        BM[HM + k, pl.ds(HY, my), :] = restrict(summed, 0.125)
    bm_halo = halo(BM, BM, (mx, my), HM, HM, med_send.at[0], med_recv.at[0], True)
    start(bm_halo)
    own_rows = pl.ds(pl.multiple_of(sub * cy, cy), cy)
    CB[box, own_rows, :] = restrict(pack([BM[HM + k, pl.ds(HY, my), :] for k in range(mx)]), 0.125)
    cb_first, cb_second = gather(CB, 0)
    for copy in cb_first:
        copy.start()
    clear(B, (nx, ny), HB, HB)
    clear(G, (nx, ny), HG, HB)
    clear(BM, (mx, my), HM, HM)
    clear(GM, (mx, my), HM, HM)
    clear(PM, (mx, my), HM, HM)

    def parity(shape):
        return (lax.broadcasted_iota(jnp.int32, shape, 0) + lax.broadcasted_iota(jnp.int32, shape, 1)) & 1

    def setup_plane(e, b_ref, x_ref, yp, ym, zp, zm, d_ref, i_ref):
        b = b_ref[e]
        lane = lax.broadcasted_iota(jnp.int32, b.shape, 1)
        half = 0.5 * b
        up, down = shifted(half, 1, 0), shifted(half, -1, 0)
        right = jnp.where(lane == b.shape[1] - 1, 0.0, shifted(half, 1, 1))
        left = jnp.where(lane == 0, 0.0, shifted(half, -1, 1))
        before, after = 0.5 * b_ref[e - 1], 0.5 * b_ref[e + 1]
        x_ref[e] = half + after
        yp[e] = half + up
        ym[e] = half + down
        zp[e] = jnp.where(lane == b.shape[1] - 1, 0.0, half + right)
        zm[e] = jnp.where(lane == 0, 0.0, half + left)
        diag = 6.0 * half + ((before + after) + (up + down) + (right + left))
        inverse = jnp.where(b > 0.0, 1.0 / diag, 0.0)
        d_ref[e] = diag
        i_ref[e] = inverse
        return inverse

    def neighbours(e, v_ref, x_ref, yp, ym, zp, zm, cut=slice(None)):
        v = v_ref[e]
        total = x_ref[e] * v_ref[e + 1] + x_ref[e - 1] * v_ref[e - 1]
        total += yp[e] * shifted(v, 1, 0) + ym[e] * shifted(v, -1, 0)
        total += zp[e] * shifted(v, 1, 1) + zm[e] * shifted(v, -1, 1)
        return total, v

    fine = (CX, CYP, CYM, CZP, CZM)
    medium = (MX, MYP, MYM, MZP, MZM)
    fine_parity, medium_parity = parity((rows, nz)), parity((mrows, mz))

    def fine_relax(colour, low, high):
        @pl.loop(low, high)
        def _(e):
            total, v = neighbours(e, V, *fine)
            V[e] = jnp.where(fine_parity == ((e + HB + colour) & 1), (G[e] + total) * I[e], v)

    def medium_relax(colour, low, high):
        @pl.loop(low, high)
        def _(e):
            total, v = neighbours(e, W, *medium)
            W[e] = jnp.where(medium_parity == ((e + HM + colour) & 1), (GM[e] + total) * IM[e], v)

    own_g.wait()
    wait_recv(beta_halo)
    wait_recv(rhs_halo)

    V[0] = jnp.zeros((rows, nz), jnp.float32)
    V[nx + 2 * HB - 1] = jnp.zeros((rows, nz), jnp.float32)

    @pl.loop(1, nx + 2 * HB - 1)
    def _(e):
        inverse = setup_plane(e, B, *fine, D, I)
        V[e] = jnp.where(fine_parity == ((e + HB) & 1), G[e] * inverse, 0.0)

    fine_relax(1, 2, nx + 2 * HB - 2)

    def fine_residual(e):
        total, v = neighbours(e, V, *fine)
        return (G[e] - (D[e] * v - total))[HY:HY + ny]

    @pl.loop(0, mx)
    def _(k):
        summed = fine_residual(HB + 2 * k) + fine_residual(HB + 2 * k + 1)
        GM[HM + k, pl.ds(HY, my), :] = restrict(summed, 0.5)

    gm_halo = halo(GM, GM, (mx, my), HM, HM, med_send.at[1], med_recv.at[1], True)
    start(gm_halo)

    wait_recv(bm_halo)
    MX[0] = 0.5 * (BM[0] + BM[1])

    @pl.loop(1, mx + 2 * HM - 1)
    def _(e):
        setup_plane(e, BM, *medium, DM, IM)

    for copy in cb_first:
        copy.wait_recv()
    for copy in cb_second:
        copy.start()
    wait_recv(gm_halo)

    @pl.loop(HM - 2, HM + mx + 2)
    def _(e):
        W[e] = jnp.where(medium_parity == ((e + HM) & 1), GM[e] * IM[e], 0.0)

    medium_relax(1, HM - 1, HM + mx + 1)
    residuals = []
    for k in range(mx):
        total, v = neighbours(HM + k, W, *medium)
        residuals.append((GM[HM + k] - (DM[HM + k] * v - total))[HY:HY + my])
        PM[HM + k, pl.ds(HY, my), :] = v[HY:HY + my]
    CR[box, own_rows, :] = restrict(pack(residuals), 0.5)
    cr_first, cr_second = gather(CR, 1)
    for copy in cr_first:
        copy.start()
    pm_halo = halo(PM, PM, (mx, my), HM, HM, med_send.at[2], med_recv.at[2], True)
    start(pm_halo)

    for copy in cb_second:
        copy.wait_recv()
    crows = ns * cy
    cz = mz // 2
    lane = lax.broadcasted_iota(jnp.int32, (crows, mz), 1)
    row = lax.broadcasted_iota(jnp.int32, (crows, mz), 0)
    low = lane < cz
    z = lane & (cz - 1)
    zero = jnp.zeros((crows, mz), jnp.float32)
    for k in range(nb):
        half = 0.5 * CB[k]
        swap = shifted(half, cz, 1)
        swap_before = 0.5 * shifted(CB[k - 1], cz, 1) if k > 0 else zero
        swap_after = 0.5 * shifted(CB[k + 1], cz, 1) if k < nb - 1 else zero
        before = jnp.where(low, swap_before, swap)
        after = jnp.where(low, swap, swap_after)
        diag = 6.0 * half + before + after
        CXM[k] = jnp.where(low, 0.0, half + before) if k == 0 else half + before
        CXP[k] = jnp.where(low, half + after, 0.0) if k == nb - 1 else half + after
        for ref, step, axis, edge in ((KYP, 1, 0, row == crows - 1), (KYM, -1, 0, row == 0),
                                      (KZP, 1, 1, z == cz - 1), (KZM, -1, 1, z == 0)):
            beside = jnp.where(edge, 0.0, shifted(half, step, axis))
            diag = diag + beside
            ref[k] = jnp.where(edge, 0.0, half + beside)
        DC[k] = diag
        IC[k] = 1.0 / diag

    XC[...] = jnp.zeros(XC.shape, jnp.float32)
    for copy in cr_first:
        copy.wait_recv()
    for copy in cr_second:
        copy.start()
    for copy in cr_second:
        copy.wait_recv()

    def total_of(value):
        return jnp.sum(jnp.sum(value, axis=0, keepdims=True), axis=1, keepdims=True)

    inner = pl.ds(HY, crows)
    acc = zero
    for k in range(nb):
        r = CR[k]
        zk = r * IC[k]
        RR[k] = r
        PP[k] = zk
        acc = acc + r * zk
    rz = total_of(acc)

    def iteration(step, rz):
        acc = zero
        images = []
        swaps = [shifted(PP[k], cz, 1) for k in range(nb)]
        for k in range(nb):
            p = PP[k]
            before = jnp.where(low, swaps[k - 1] if k > 0 else zero, swaps[k])
            after = jnp.where(low, swaps[k], swaps[k + 1] if k < nb - 1 else zero)
            total = CXM[k] * before + CXP[k] * after
            total += KYP[k] * shifted(p, 1, 0) + KYM[k] * shifted(p, -1, 0)
            total += KZP[k] * shifted(p, 1, 1) + KZM[k] * shifted(p, -1, 1)
            q = DC[k] * p - total
            images.append(q)
            acc = acc + p * q
        alpha = rz / total_of(acc)
        acc = zero
        preconds = []
        for k in range(nb):
            XC[k + 1, inner, :] += alpha * PP[k]
            r = RR[k] - alpha * images[k]
            RR[k] = r
            zk = r * IC[k]
            preconds.append(zk)
            acc = acc + r * zk
        new = total_of(acc)
        ratio = new / rz
        for k in range(nb):
            PP[k] = preconds[k] + ratio * PP[k]
        return new

    lax.fori_loop(0, ITERS, iteration, rz)

    wait_recv(pm_halo)
    window = pl.ds(pl.multiple_of(sub * cy, cy), cy + 2 * HY)
    for j in range(3):
        part = XC[box + j, window, :]
        wide = jnp.dot(part, spread, precision=HIGHEST, preferred_element_type=jnp.float32)
        for side in range(2):
            plane = wide[HY // 2:HY // 2 + mrows // 2, side * mz:(side + 1) * mz]
            TMP[pl.ds(0, mrows // 2, stride=2), :] = plane
            TMP[pl.ds(1, mrows // 2, stride=2), :] = plane
            copied = TMP[0:mrows, :]
            for twin in range(2):
                e = 4 * j + 2 * side + twin
                W[e] = PM[e] + copied
    medium_relax(0, 1, mx + 2 * HM - 1)
    medium_relax(1, 2, mx + 2 * HM - 2)

    for k in range(-2, mx + 2):
        plane = W[HM + k, pl.ds(HY // 2, rows // 2), :]
        TMP[pl.ds(0, rows // 2, stride=2), :] = plane
        TMP[pl.ds(1, rows // 2, stride=2), :] = plane
        wide = jnp.dot(TMP[0:rows, :], spread, precision=HIGHEST, preferred_element_type=jnp.float32)
        for e in (HB + 2 * k, HB + 2 * k + 1):
            V[e] = V[e] + wide
    fine_relax(0, HB - 2, HB + nx + 2)
    fine_relax(1, HB - 1, HB + nx + 1)

    @pl.loop(0, nx)
    def _(k):
        e = HB + k
        r_out[k] = fine_residual(e)
        p_out[k] = V[e, pl.ds(HY, ny), :]

    for copies in (beta_halo, rhs_halo, bm_halo, gm_halo, pm_halo):
        wait_send(copies)
    for copies in (cb_first, cb_second, cr_first, cr_second):
        for copy in copies:
            copy.wait_send()


def solution(mesh):
    nb, ns = mesh.shape["box"], mesh.shape["sub"]

    def shards(right_side, beta):
        nx, ny, nz = right_side.shape
        mx, my, mz = nx // 2, ny // 2, nz // 2
        fine = (nx + 2 * HB, ny + 2 * HY, nz)
        medium = (mx + 2 * HM, my + 2 * HY, mz)
        coarse = (nb, ns * (my // 2), mz)
        vmem = lambda shape, count: [pltpu.VMEM(shape, jnp.float32)] * count
        sems = pltpu.SemaphoreType.DMA
        return pl.pallas_call(
            functools.partial(kernel, nb, ns),
            out_shape=[jax.ShapeDtypeStruct((nx, ny, nz), jnp.float32)] * 2,
            in_specs=[pl.BlockSpec(memory_space=pl.ANY)] * 2,
            out_specs=[pl.BlockSpec(memory_space=pltpu.VMEM)] * 2,
            scratch_shapes=(
                vmem(fine, 10) + vmem((ny + 2 * HY, mz), 1) + vmem(medium, 11) + vmem(coarse, 2)
                + vmem((nb + 2, ns * (my // 2) + 2 * HY, mz), 1) + vmem(coarse, 8) + vmem(coarse, 2)
                + [sems((2,)), sems((2, 8)), sems((2, 8)), sems((3, 8)), sems((3, 8)),
                   sems((2, nb - 1)), sems((2, nb - 1)), sems((2, ns - 1)), sems((2, ns - 1))]),
            compiler_params=pltpu.CompilerParams(
                has_side_effects=True, vmem_limit_bytes=48 * 1024 * 1024),
        )(right_side, beta)

    placed = (P("box", "sub", None), P("box", "sub", None))
    return jax.shard_map(shards, mesh=mesh, in_specs=placed, out_specs=placed, check_vma=False)
```

time: 1020 us -> 53.4 us (0.05)
  blocking collectives: 617 us -> 0 us
  starting transfers between devices: 182 us -> 0 us
  waiting for transfers between devices: 109 us -> 0 us
  Pallas kernels: 0 us -> 49.3 us
  local copies, waits for them, and re-layouts: 46.7 us -> 3.3 us
  other arithmetic: 34.2 us -> 0 us
  between operations: 22.3 us -> 0.65 us
    psum x15 -> x0, blocking collectives: 617 us -> none  [the longest x8 331 us: norm_total(): return lax.psum(value, ('box', 'sub'))]
    ppermute x80 -> x0, starting transfers between devices: 182 us -> none  [the longest x40 130 us: with_halo(): before = lax.ppermute(last, axis, up)]
    ppermute x80 -> x0, waiting for transfers between devices: 109 us -> none  [the longest x40 109 us: with_halo(): after = lax.ppermute(first, axis, down)]
    pallas_call x0 -> x1, Pallas kernels: none -> 49.3 us  [shards(): pl.pallas_call(functools.partial(kernel, nb, ns), out_shape=[jax.ShapeDty...]
    reshape x7 -> x0, local copies, waits for them, and re-layouts: 41.1 us -> none  [the longest x3 40.3 us: restrict(): field.reshape(nx // 2, 2, ny // 2, 2, nz // 2, 2).sum(axis=(1, 3, 5))]
    reduce_sum x19 -> x0, other arithmetic: 27.3 us -> none  [the longest x4 17.6 us: restrict(): field.reshape(nx // 2, 2, ny // 2, 2, nz // 2, 2).sum(axis=(1, 3, 5))]
  transfers between devices with their start and end apart: 80 -> 0, of which waited for: 34 -> 0; matrix products, arithmetic and copies ran while one was open for 3% -> 0% of each run, Pallas kernels for 0% -> 0%
where the time goes in v1:
time: 53.4 us; the launch traced here: 53.2 us
  Pallas kernels  49.3 us (92%)
  local copies, waits for them, and re-layouts  3.3 us (6%)
  between operations  0.65 us (1%)
    pallas_call x1, Pallas kernels, shards(): pl.pallas_call(functools.partial(kernel, nb, ns), out_shape=[jax.ShapeDty...  49.3 us
    unnamed x6, local copies, waits for them, and re-layouts  3.3 us

profile of v1, /device:TPU:0, one launch (start us, length us, event | category | flops | bytes accessed | tf_op | source)
XLA Modules:
  0.0 53.2 jit_solution(15004182243576434702)
XLA Ops:
  0.6 0.0 copy-start
  0.6 0.9 %copy-done = f32[8,32,256]{2,1,0:T(8,128)S(1)} copy-done((f32[8,32,256]{2,1,0:T(8,128)S(1)}, f32[8,32,256]{2,1,0:T(8,128)}, u32[]{:S(2)}) %copy-start) | copy-done | bytes 262168
  1.6 0.0 copy-start.1
  1.6 0.9 %copy-done.1 = f32[8,32,256]{2,1,0:T(8,128)S(1)} copy-done((f32[8,32,256]{2,1,0:T(8,128)S(1)}, f32[8,32,256]{2,1,0:T(8,128)}, u32[]{:S(2)}) %copy-start.1) | copy-done | bytes 262168
  2.5 49.3 %shard_map.41 = (f32[8,32,256]{2,1,0:T(8,128)S(1)}, f32[8,32,256]{2,1,0:T(8,128)S(1)}) custom-call(f32[8,32,256]{2,1,0:T(8,128)S(1)} %copy-done, f32[8,32,256]{2,1,0:T(8,128)S(1)} %copy-done.1), custom_call_target="tpu_custom_call" | custom-call | tf_op jit(solution)/shard_map/pallas_call | solution.py:368
  51.8 0.7 %copy.6 = f32[8,32,256]{2,1,0:T(8,128)} copy(f32[8,32,256]{2,1,0:T(8,128)S(1)} %get-tuple-element.4) | data formatting | bytes 524288
  52.5 0.7 %copy.7 = f32[8,32,256]{2,1,0:T(8,128)} copy(f32[8,32,256]{2,1,0:T(8,128)S(1)} %get-tuple-element.5) | data formatting | bytes 524288
Async XLA Ops:
  0.6 1.0 %copy-start = (f32[8,32,256]{2,1,0:T(8,128)S(1)}, f32[8,32,256]{2,1,0:T(8,128)}, u32[]{:S(2)}) copy-start(f32[8,32,256]{2,1,0:T(8,128)} %g_in.1) | copy-start | bytes 786436
  1.6 0.9 %copy-start.1 = (f32[8,32,256]{2,1,0:T(8,128)S(1)}, f32[8,32,256]{2,1,0:T(8,128)}, u32[]{:S(2)}) copy-start(f32[8,32,256]{2,1,0:T(8,128)} %b_in.1) | copy-start | bytes 786436

commit v2 on v1

--- a/solution.py
+++ b/solution.py
@@ -8,10 +8,11 @@
 from jax.sharding import PartitionSpec as P
 
 ITERS = 8
-HB = 5
-HG = 4
+HB = 3
+HG = 2
+HM = 4
+HR = 3
 HY = 8
-HM = 4
 DIRECTIONS = [(dx, dy) for dx in (-1, 0, 1) for dy in (-1, 0, 1) if (dx, dy) != (0, 0)]
 HIGHEST = lax.Precision.HIGHEST
 
@@ -28,9 +29,9 @@
     return pltpu.roll(value, (-step) % value.shape[axis], axis)
 
 
-def kernel(nb, ns, g_in, b_in, p_out, r_out, B, G, CX, CYP, CYM, CZP, CZM, D, I, V, TMP,
+def kernel(nb, ns, g_in, b_in, p_out, r_out, B, G, CX, CYP, CYM, CZP, CZM, D, I, V, VP, TMP,
            BM, GM, MX, MYP, MYM, MZP, MZM, DM, IM, W, PM, CB, CR, XC, CXP, CXM, KYP, KYM, KZP, KZM, DC, IC,
-           RR, PP, own_sem, fine_send, fine_recv, med_send, med_recv, box_send, box_recv, sub_send, sub_recv):
+           RR, PP, own_sem, fine_send, fine_recv, med_send, med_recv, all_send, all_recv):
     nx, ny, nz = g_in.shape
     mx, my, mz = nx // 2, ny // 2, nz // 2
     cy = my // 2
@@ -44,10 +45,11 @@
             ok = here if ok is None else (ok if here is None else jnp.logical_and(ok, here))
         return ok
 
-    def halo(src, dst, own, width_x, halo_x, sends, recvs, from_ext):
+    def halo(src, dst, own, width, halo_x, sends, recvs, from_ext):
         out = []
         for k, (dx, dy) in enumerate(DIRECTIONS):
-            sx, tx, lx = span(dx, own[0], width_x, halo_x)
+            deep = width - 1 if dx and dy else width
+            sx, tx, lx = span(dx, own[0], deep, halo_x)
             sy, ty, ly = span(dy, own[1], HY, HY)
             if from_ext:
                 sx, sy = sx + halo_x, sy + HY
@@ -71,9 +73,10 @@
         for (dx, dy), copy in zip(DIRECTIONS, copies):
             pl.when(exists(dx, dy))(copy.wait_send)
 
-    def clear(dst, own, width_x, halo_x):
+    def clear(dst, own, width, halo_x):
         for dx, dy in DIRECTIONS:
-            _, tx, lx = span(dx, own[0], width_x, halo_x)
+            deep = width - 1 if dx and dy else width
+            _, tx, lx = span(dx, own[0], deep, halo_x)
             _, ty, ly = span(dy, own[1], HY, HY)
 
             @pl.when(jnp.logical_not(exists(-dx, -dy)))
@@ -85,9 +88,17 @@
     own_b = pltpu.make_async_copy(b_in, B.at[pl.ds(HB, nx), pl.ds(HY, ny), :], own_sem.at[0])
     own_g = pltpu.make_async_copy(g_in, G.at[pl.ds(HB, nx), pl.ds(HY, ny), :], own_sem.at[1])
     own_b.start()
-    start(beta_halo)
-    start(rhs_halo)
     own_g.start()
+
+    count = nb * ns
+
+    def peer(k):
+        return {"box": lax.rem(box + k // ns, nb), "sub": lax.rem(sub + k % ns, ns)}
+
+    barrier = pltpu.get_barrier_semaphore()
+
+    for k in range(1, count):
+        pl.semaphore_signal(barrier, inc=1, device_id=peer(k), device_id_type=pl.DeviceIdType.MESH)
 
     pair_sum = (lax.broadcasted_iota(jnp.int32, (nz, mz), 0) >> 1
                 == lax.broadcasted_iota(jnp.int32, (nz, mz), 1)).astype(jnp.float32)
@@ -102,37 +113,39 @@
     def pack(planes):
         return jnp.concatenate([planes[0] + planes[1], planes[2] + planes[3]], axis=1)
 
+    own_rows = pl.ds(pl.multiple_of(sub * cy, cy), cy)
+
     def gather(buffer, index):
-        def block(b, s, size):
-            return buffer.at[pl.ds(b, size), pl.ds(pl.multiple_of(s * cy, cy), cy), :]
-        first = [pltpu.make_async_remote_copy(
-            src_ref=block(box, sub, 1), dst_ref=block(box, sub, 1),
-            send_sem=box_send.at[index, k], recv_sem=box_recv.at[index, k],
-            device_id={"box": lax.rem(box + k + 1, nb), "sub": sub}, device_id_type=pl.DeviceIdType.MESH)
-            for k in range(nb - 1)]
-        second = [pltpu.make_async_remote_copy(
-            src_ref=block(0, sub, nb), dst_ref=block(0, sub, nb),
-            send_sem=sub_send.at[index, k], recv_sem=sub_recv.at[index, k],
-            device_id={"box": box, "sub": lax.rem(sub + k + 1, ns)}, device_id_type=pl.DeviceIdType.MESH)
-            for k in range(ns - 1)]
-        return first, second
+        def copy(k):
+            block = buffer.at[pl.ds(box, 1), own_rows, :]
+            return pltpu.make_async_remote_copy(
+                src_ref=block, dst_ref=block, send_sem=all_send.at[index, k - 1], recv_sem=all_recv.at[index, k - 1],
+                device_id=peer(k), device_id_type=pl.DeviceIdType.MESH)
+
+        def over(action):
+            for k in range(1, count):
+                action(copy(k))
+        return over
+
+    gather_b, gather_r = gather(CB, 0), gather(CR, 1)
 
     own_b.wait()
     for k in range(mx):
         summed = B[HB + 2 * k, pl.ds(HY, ny), :] + B[HB + 2 * k + 1, pl.ds(HY, ny), :]
         BM[HM + k, pl.ds(HY, my), :] = restrict(summed, 0.125)
+    CB[box, own_rows, :] = restrict(pack([BM[HM + k, pl.ds(HY, my), :] for k in range(mx)]), 0.125)
+    pl.semaphore_wait(barrier, count - 1)
+    start(beta_halo)
+    start(rhs_halo)
     bm_halo = halo(BM, BM, (mx, my), HM, HM, med_send.at[0], med_recv.at[0], True)
     start(bm_halo)
-    own_rows = pl.ds(pl.multiple_of(sub * cy, cy), cy)
-    CB[box, own_rows, :] = restrict(pack([BM[HM + k, pl.ds(HY, my), :] for k in range(mx)]), 0.125)
-    cb_first, cb_second = gather(CB, 0)
-    for copy in cb_first:
-        copy.start()
     clear(B, (nx, ny), HB, HB)
     clear(G, (nx, ny), HG, HB)
+    clear(VP, (nx, ny), HB, HB)
     clear(BM, (mx, my), HM, HM)
-    clear(GM, (mx, my), HM, HM)
+    clear(GM, (mx, my), HR, HM)
     clear(PM, (mx, my), HM, HM)
+    gather_b(lambda copy: copy.start())
 
     def parity(shape):
         return (lax.broadcasted_iota(jnp.int32, shape, 0) + lax.broadcasted_iota(jnp.int32, shape, 1)) & 1
@@ -183,8 +196,7 @@
     wait_recv(beta_halo)
     wait_recv(rhs_halo)
 
-    V[0] = jnp.zeros((rows, nz), jnp.float32)
-    V[nx + 2 * HB - 1] = jnp.zeros((rows, nz), jnp.float32)
+    CX[0] = 0.5 * (B[0] + B[1])
 
     @pl.loop(1, nx + 2 * HB - 1)
     def _(e):
@@ -200,10 +212,14 @@
     @pl.loop(0, mx)
     def _(k):
         summed = fine_residual(HB + 2 * k) + fine_residual(HB + 2 * k + 1)
+        VP[HB + 2 * k, pl.ds(HY, ny), :] = V[HB + 2 * k, pl.ds(HY, ny), :]
+        VP[HB + 2 * k + 1, pl.ds(HY, ny), :] = V[HB + 2 * k + 1, pl.ds(HY, ny), :]
         GM[HM + k, pl.ds(HY, my), :] = restrict(summed, 0.5)
 
-    gm_halo = halo(GM, GM, (mx, my), HM, HM, med_send.at[1], med_recv.at[1], True)
+    gm_halo = halo(GM, GM, (mx, my), HR, HM, med_send.at[1], med_recv.at[1], True)
     start(gm_halo)
+    pre_halo = halo(VP, VP, (nx, ny), HB, HB, fine_send.at[2], fine_recv.at[2], True)
+    start(pre_halo)
 
     wait_recv(bm_halo)
     MX[0] = 0.5 * (BM[0] + BM[1])
@@ -212,10 +228,6 @@
     def _(e):
         setup_plane(e, BM, *medium, DM, IM)
 
-    for copy in cb_first:
-        copy.wait_recv()
-    for copy in cb_second:
-        copy.start()
     wait_recv(gm_halo)
 
     @pl.loop(HM - 2, HM + mx + 2)
@@ -229,14 +241,11 @@
         residuals.append((GM[HM + k] - (DM[HM + k] * v - total))[HY:HY + my])
         PM[HM + k, pl.ds(HY, my), :] = v[HY:HY + my]
     CR[box, own_rows, :] = restrict(pack(residuals), 0.5)
-    cr_first, cr_second = gather(CR, 1)
-    for copy in cr_first:
-        copy.start()
+    gather_r(lambda copy: copy.start())
     pm_halo = halo(PM, PM, (mx, my), HM, HM, med_send.at[2], med_recv.at[2], True)
     start(pm_halo)
 
-    for copy in cb_second:
-        copy.wait_recv()
+    gather_b(lambda copy: copy.wait_recv())
     crows = ns * cy
     cz = mz // 2
     lane = lax.broadcasted_iota(jnp.int32, (crows, mz), 1)
@@ -263,12 +272,7 @@
         IC[k] = 1.0 / diag
 
     XC[...] = jnp.zeros(XC.shape, jnp.float32)
-    for copy in cr_first:
-        copy.wait_recv()
-    for copy in cr_second:
-        copy.start()
-    for copy in cr_second:
-        copy.wait_recv()
+    gather_r(lambda copy: copy.wait_recv())
 
     def total_of(value):
         return jnp.sum(jnp.sum(value, axis=0, keepdims=True), axis=1, keepdims=True)
@@ -331,13 +335,15 @@
     medium_relax(0, 1, mx + 2 * HM - 1)
     medium_relax(1, 2, mx + 2 * HM - 2)
 
+    wait_recv(pre_halo)
     for k in range(-2, mx + 2):
         plane = W[HM + k, pl.ds(HY // 2, rows // 2), :]
         TMP[pl.ds(0, rows // 2, stride=2), :] = plane
         TMP[pl.ds(1, rows // 2, stride=2), :] = plane
         wide = jnp.dot(TMP[0:rows, :], spread, precision=HIGHEST, preferred_element_type=jnp.float32)
         for e in (HB + 2 * k, HB + 2 * k + 1):
-            V[e] = V[e] + wide
+            if 0 <= e < nx + 2 * HB:
+                V[e] = VP[e] + wide
     fine_relax(0, HB - 2, HB + nx + 2)
     fine_relax(1, HB - 1, HB + nx + 1)
 
@@ -347,11 +353,10 @@
         r_out[k] = fine_residual(e)
         p_out[k] = V[e, pl.ds(HY, ny), :]
 
-    for copies in (beta_halo, rhs_halo, bm_halo, gm_halo, pm_halo):
+    for copies in (beta_halo, rhs_halo, bm_halo, gm_halo, pm_halo, pre_halo):
         wait_send(copies)
-    for copies in (cb_first, cb_second, cr_first, cr_second):
-        for copy in copies:
-            copy.wait_send()
+    gather_b(lambda copy: copy.wait_send())
+    gather_r(lambda copy: copy.wait_send())
 
 
 def solution(mesh):
@@ -368,15 +373,15 @@
         return pl.pallas_call(
             functools.partial(kernel, nb, ns),
             out_shape=[jax.ShapeDtypeStruct((nx, ny, nz), jnp.float32)] * 2,
-            in_specs=[pl.BlockSpec(memory_space=pl.ANY)] * 2,
+            in_specs=[pl.BlockSpec(memory_space=pltpu.HBM)] * 2,
             out_specs=[pl.BlockSpec(memory_space=pltpu.VMEM)] * 2,
             scratch_shapes=(
-                vmem(fine, 10) + vmem((ny + 2 * HY, mz), 1) + vmem(medium, 11) + vmem(coarse, 2)
+                vmem(fine, 11) + vmem((ny + 2 * HY, mz), 1) + vmem(medium, 11) + vmem(coarse, 2)
                 + vmem((nb + 2, ns * (my // 2) + 2 * HY, mz), 1) + vmem(coarse, 8) + vmem(coarse, 2)
-                + [sems((2,)), sems((2, 8)), sems((2, 8)), sems((3, 8)), sems((3, 8)),
-                   sems((2, nb - 1)), sems((2, nb - 1)), sems((2, ns - 1)), sems((2, ns - 1))]),
+                + [sems((2,)), sems((3, 8)), sems((3, 8)), sems((3, 8)), sems((3, 8)),
+                   sems((2, nb * ns - 1)), sems((2, nb * ns - 1))]),
             compiler_params=pltpu.CompilerParams(
-                has_side_effects=True, vmem_limit_bytes=48 * 1024 * 1024),
+                collective_id=0, has_side_effects=True, vmem_limit_bytes=48 * 1024 * 1024),
         )(right_side, beta)
 
     placed = (P("box", "sub", None), P("box", "sub", None))

time: 53.4 us -> 45.6 us (0.85)
  Pallas kernels: 49.3 us -> 41.5 us
    pallas_call x1, Pallas kernels: 49.3 us -> 41.5 us  [shards(): pl.pallas_call(functools.partial(kernel, nb, ns), out_shape=[jax.ShapeDty...]
where the time goes in v2:
time: 45.6 us; the launch traced here: 45.5 us
  Pallas kernels  41.5 us (91%)
  local copies, waits for them, and re-layouts  3.3 us (7%)
  between operations  0.65 us (1%)
    pallas_call x1, Pallas kernels, shards(): pl.pallas_call(functools.partial(kernel, nb, ns), out_shape=[jax.ShapeDty...  41.5 us
    unnamed x6, local copies, waits for them, and re-layouts  3.3 us

profile of v2, /device:TPU:0, one launch (start us, length us, event | category | flops | bytes accessed | tf_op | source)
XLA Modules:
  0.0 45.5 jit_solution(8327407303456909521)
XLA Ops:
  0.6 0.0 copy-start
  0.6 0.9 %copy-done = f32[8,32,256]{2,1,0:T(8,128)S(1)} copy-done((f32[8,32,256]{2,1,0:T(8,128)S(1)}, f32[8,32,256]{2,1,0:T(8,128)}, u32[]{:S(2)}) %copy-start) | copy-done | bytes 262168
  1.6 0.0 copy-start.1
  1.6 0.9 %copy-done.1 = f32[8,32,256]{2,1,0:T(8,128)S(1)} copy-done((f32[8,32,256]{2,1,0:T(8,128)S(1)}, f32[8,32,256]{2,1,0:T(8,128)}, u32[]{:S(2)}) %copy-start.1) | copy-done | bytes 262168
  2.5 41.5 %shard_map.41 = (f32[8,32,256]{2,1,0:T(8,128)S(1)}, f32[8,32,256]{2,1,0:T(8,128)S(1)}) custom-call(f32[8,32,256]{2,1,0:T(8,128)S(1)} %copy-done, f32[8,32,256]{2,1,0:T(8,128)S(1)} %copy-done.1), custom_call_target="tpu_custom_call" | custom-call | tf_op jit(solution)/shard_map/pallas_call | solution.py:373
  44.1 0.7 %copy.6 = f32[8,32,256]{2,1,0:T(8,128)} copy(f32[8,32,256]{2,1,0:T(8,128)S(1)} %get-tuple-element.4) | data formatting | bytes 524288
  44.8 0.7 %copy.7 = f32[8,32,256]{2,1,0:T(8,128)} copy(f32[8,32,256]{2,1,0:T(8,128)S(1)} %get-tuple-element.5) | data formatting | bytes 524288
Async XLA Ops:
  0.6 1.0 %copy-start = (f32[8,32,256]{2,1,0:T(8,128)S(1)}, f32[8,32,256]{2,1,0:T(8,128)}, u32[]{:S(2)}) copy-start(f32[8,32,256]{2,1,0:T(8,128)} %g_in.1) | copy-start | bytes 786436
  1.6 0.9 %copy-start.1 = (f32[8,32,256]{2,1,0:T(8,128)S(1)}, f32[8,32,256]{2,1,0:T(8,128)}, u32[]{:S(2)}) copy-start(f32[8,32,256]{2,1,0:T(8,128)} %b_in.1) | copy-start | bytes 786436

commit v3 on v2

--- a/solution.py
+++ b/solution.py
@@ -29,7 +29,7 @@
     return pltpu.roll(value, (-step) % value.shape[axis], axis)
 
 
-def kernel(nb, ns, g_in, b_in, p_out, r_out, B, G, CX, CYP, CYM, CZP, CZM, D, I, V, VP, TMP,
+def kernel(nb, ns, g_in, b_in, p_out, r_out, B, G, CX, CYP, CYM, CZP, CZM, D, I, V, VP, PS, PR, TMP,
            BM, GM, MX, MYP, MYM, MZP, MZM, DM, IM, W, PM, CB, CR, XC, CXP, CXM, KYP, KYM, KZP, KZM, DC, IC,
            RR, PP, own_sem, fine_send, fine_recv, med_send, med_recv, all_send, all_recv):
     nx, ny, nz = g_in.shape
@@ -45,9 +45,12 @@
             ok = here if ok is None else (ok if here is None else jnp.logical_and(ok, here))
         return ok
 
-    def halo(src, dst, own, width, halo_x, sends, recvs, from_ext):
+    def halo(src, dst, own, width, halo_x, sends, recvs, from_ext, flat=False):
         out = []
         for k, (dx, dy) in enumerate(DIRECTIONS):
+            if flat and dy:
+                out.append(None)
+                continue
             deep = width - 1 if dx and dy else width
             sx, tx, lx = span(dx, own[0], deep, halo_x)
             sy, ty, ly = span(dy, own[1], HY, HY)
@@ -63,18 +66,42 @@
 
     def start(copies):
         for (dx, dy), copy in zip(DIRECTIONS, copies):
-            pl.when(exists(dx, dy))(copy.start)
+            if copy is not None:
+                pl.when(exists(dx, dy))(copy.start)
 
     def wait_recv(copies):
         for (dx, dy), copy in zip(DIRECTIONS, copies):
-            pl.when(exists(-dx, -dy))(copy.wait_recv)
+            if copy is not None:
+                pl.when(exists(-dx, -dy))(copy.wait_recv)
 
     def wait_send(copies):
         for (dx, dy), copy in zip(DIRECTIONS, copies):
-            pl.when(exists(dx, dy))(copy.wait_send)
-
-    def clear(dst, own, width, halo_x):
+            if copy is not None:
+                pl.when(exists(dx, dy))(copy.wait_send)
+
+    def packed_halo(sends, recvs):
+        out = []
+        for k, (dx, dy) in enumerate(DIRECTIONS):
+            if dy == 0:
+                out.append(None)
+                continue
+            sx, tx, lx = span(dx, nx, HB - 1, HB)
+            at = 0 if dy > 0 else 1
+            out.append(pltpu.make_async_remote_copy(
+                src_ref=PS.at[at, pl.ds(sx, lx), :, :], dst_ref=PR.at[at, pl.ds(tx, lx), :, :],
+                send_sem=sends.at[k], recv_sem=recvs.at[k],
+                device_id={"box": box + dx, "sub": sub + dy},
+                device_id_type=pl.DeviceIdType.MESH))
+
+            @pl.when(jnp.logical_not(exists(-dx, -dy)))
+            def _():
+                PR[at, pl.ds(tx, lx), :, :] = jnp.zeros((lx, HY, nz), jnp.float32)
+        return out
+
+    def clear(dst, own, width, halo_x, flat=False):
         for dx, dy in DIRECTIONS:
+            if flat and dy:
+                continue
             deep = width - 1 if dx and dy else width
             _, tx, lx = span(dx, own[0], deep, halo_x)
             _, ty, ly = span(dy, own[1], HY, HY)
@@ -83,8 +110,8 @@
             def _():
                 dst[pl.ds(tx, lx), pl.ds(ty, ly), :] = jnp.zeros((lx, ly, dst.shape[2]), jnp.float32)
 
-    beta_halo = halo(b_in, B, (nx, ny), HB, HB, fine_send.at[0], fine_recv.at[0], False)
-    rhs_halo = halo(g_in, G, (nx, ny), HG, HB, fine_send.at[1], fine_recv.at[1], False)
+    beta_halo = halo(b_in, B, (nx, ny), HB, HB, fine_send.at[0], fine_recv.at[0], False, True)
+    rhs_halo = halo(g_in, G, (nx, ny), HG, HB, fine_send.at[1], fine_recv.at[1], False, True)
     own_b = pltpu.make_async_copy(b_in, B.at[pl.ds(HB, nx), pl.ds(HY, ny), :], own_sem.at[0])
     own_g = pltpu.make_async_copy(g_in, G.at[pl.ds(HB, nx), pl.ds(HY, ny), :], own_sem.at[1])
     own_b.start()
@@ -134,13 +161,21 @@
         summed = B[HB + 2 * k, pl.ds(HY, ny), :] + B[HB + 2 * k + 1, pl.ds(HY, ny), :]
         BM[HM + k, pl.ds(HY, my), :] = restrict(summed, 0.125)
     CB[box, own_rows, :] = restrict(pack([BM[HM + k, pl.ds(HY, my), :] for k in range(mx)]), 0.125)
+    own_g.wait()
+    tile_row = lax.broadcasted_iota(jnp.int32, (HY, nz), 0)
+    for e in range(nx):
+        for at, edge, mine in ((0, ny, tile_row >= HY - HB), (1, HY, tile_row < HB)):
+            rhs = pltpu.roll(G[HB + e, pl.ds(edge, HY), :], HY // 2, 0)
+            PS[at, e] = jnp.where(mine, B[HB + e, pl.ds(edge, HY), :], rhs)
+    pack_halo = packed_halo(fine_send.at[3], fine_recv.at[3])
     pl.semaphore_wait(barrier, count - 1)
+    start(pack_halo)
     start(beta_halo)
     start(rhs_halo)
     bm_halo = halo(BM, BM, (mx, my), HM, HM, med_send.at[0], med_recv.at[0], True)
     start(bm_halo)
-    clear(B, (nx, ny), HB, HB)
-    clear(G, (nx, ny), HG, HB)
+    clear(B, (nx, ny), HB, HB, True)
+    clear(G, (nx, ny), HG, HB, True)
     clear(VP, (nx, ny), HB, HB)
     clear(BM, (mx, my), HM, HM)
     clear(GM, (mx, my), HR, HM)
@@ -192,9 +227,14 @@
             total, v = neighbours(e, W, *medium)
             W[e] = jnp.where(medium_parity == ((e + HM + colour) & 1), (GM[e] + total) * IM[e], v)
 
-    own_g.wait()
     wait_recv(beta_halo)
     wait_recv(rhs_halo)
+    wait_recv(pack_halo)
+    for e in range(1, nx + 2 * HB - 1):
+        for at, edge in ((0, 0), (1, HY + ny)):
+            both = PR[at, e]
+            B[e, pl.ds(edge, HY), :] = both
+            G[e, pl.ds(edge, HY), :] = pltpu.roll(both, HY // 2, 0)
 
     CX[0] = 0.5 * (B[0] + B[1])
 
@@ -353,7 +393,7 @@
         r_out[k] = fine_residual(e)
         p_out[k] = V[e, pl.ds(HY, ny), :]
 
-    for copies in (beta_halo, rhs_halo, bm_halo, gm_halo, pm_halo, pre_halo):
+    for copies in (beta_halo, rhs_halo, bm_halo, gm_halo, pm_halo, pre_halo, pack_halo):
         wait_send(copies)
     gather_b(lambda copy: copy.wait_send())
     gather_r(lambda copy: copy.wait_send())
@@ -376,9 +416,9 @@
             in_specs=[pl.BlockSpec(memory_space=pltpu.HBM)] * 2,
             out_specs=[pl.BlockSpec(memory_space=pltpu.VMEM)] * 2,
             scratch_shapes=(
-                vmem(fine, 11) + vmem((ny + 2 * HY, mz), 1) + vmem(medium, 11) + vmem(coarse, 2)
+                vmem(fine, 11) + vmem((2, nx, HY, nz), 1) + vmem((2, nx + 2 * HB, HY, nz), 1) + vmem((ny + 2 * HY, mz), 1) + vmem(medium, 11) + vmem(coarse, 2)
                 + vmem((nb + 2, ns * (my // 2) + 2 * HY, mz), 1) + vmem(coarse, 8) + vmem(coarse, 2)
-                + [sems((2,)), sems((3, 8)), sems((3, 8)), sems((3, 8)), sems((3, 8)),
+                + [sems((2,)), sems((4, 8)), sems((4, 8)), sems((3, 8)), sems((3, 8)),
                    sems((2, nb * ns - 1)), sems((2, nb * ns - 1))]),
             compiler_params=pltpu.CompilerParams(
                 collective_id=0, has_side_effects=True, vmem_limit_bytes=48 * 1024 * 1024),

time: 45.6 us -> 42 us (0.921)
  Pallas kernels: 41.5 us -> 37.9 us
    pallas_call x1, Pallas kernels: 41.5 us -> 37.9 us  [shards(): pl.pallas_call(functools.partial(kernel, nb, ns), out_shape=[jax.ShapeDty...]
where the time goes in v3:
time: 42 us; the launch traced here: 41.8 us
  Pallas kernels  37.9 us (90%)
  local copies, waits for them, and re-layouts  3.3 us (8%)
  between operations  0.65 us (2%)
    pallas_call x1, Pallas kernels, shards(): pl.pallas_call(functools.partial(kernel, nb, ns), out_shape=[jax.ShapeDty...  37.9 us
    unnamed x6, local copies, waits for them, and re-layouts  3.3 us

profile of v3, /device:TPU:0, one launch (start us, length us, event | category | flops | bytes accessed | tf_op | source)
XLA Modules:
  0.0 41.8 jit_solution(10823898234465859662)
XLA Ops:
  0.6 0.0 copy-start
  0.6 0.9 %copy-done = f32[8,32,256]{2,1,0:T(8,128)S(1)} copy-done((f32[8,32,256]{2,1,0:T(8,128)S(1)}, f32[8,32,256]{2,1,0:T(8,128)}, u32[]{:S(2)}) %copy-start) | copy-done | bytes 262168
  1.6 0.0 copy-start.1
  1.6 0.9 %copy-done.1 = f32[8,32,256]{2,1,0:T(8,128)S(1)} copy-done((f32[8,32,256]{2,1,0:T(8,128)S(1)}, f32[8,32,256]{2,1,0:T(8,128)}, u32[]{:S(2)}) %copy-start.1) | copy-done | bytes 262168
  2.5 37.9 %shard_map.41 = (f32[8,32,256]{2,1,0:T(8,128)S(1)}, f32[8,32,256]{2,1,0:T(8,128)S(1)}) custom-call(f32[8,32,256]{2,1,0:T(8,128)S(1)} %copy-done, f32[8,32,256]{2,1,0:T(8,128)S(1)} %copy-done.1), custom_call_target="tpu_custom_call" | custom-call | tf_op jit(solution)/shard_map/pallas_call | solution.py:413
  40.4 0.7 %copy.6 = f32[8,32,256]{2,1,0:T(8,128)} copy(f32[8,32,256]{2,1,0:T(8,128)S(1)} %get-tuple-element.4) | data formatting | bytes 524288
  41.1 0.7 %copy.7 = f32[8,32,256]{2,1,0:T(8,128)} copy(f32[8,32,256]{2,1,0:T(8,128)S(1)} %get-tuple-element.5) | data formatting | bytes 524288
Async XLA Ops:
  0.6 1.0 %copy-start = (f32[8,32,256]{2,1,0:T(8,128)S(1)}, f32[8,32,256]{2,1,0:T(8,128)}, u32[]{:S(2)}) copy-start(f32[8,32,256]{2,1,0:T(8,128)} %g_in.1) | copy-start | bytes 786436
  1.6 0.9 %copy-start.1 = (f32[8,32,256]{2,1,0:T(8,128)S(1)}, f32[8,32,256]{2,1,0:T(8,128)}, u32[]{:S(2)}) copy-start(f32[8,32,256]{2,1,0:T(8,128)} %b_in.1) | copy-start | bytes 786436

commit v4 on v3

--- a/solution.py
+++ b/solution.py
@@ -180,7 +180,6 @@
     clear(BM, (mx, my), HM, HM)
     clear(GM, (mx, my), HR, HM)
     clear(PM, (mx, my), HM, HM)
-    gather_b(lambda copy: copy.start())
 
     def parity(shape):
         return (lax.broadcasted_iota(jnp.int32, shape, 0) + lax.broadcasted_iota(jnp.int32, shape, 1)) & 1
@@ -258,8 +257,8 @@
 
     gm_halo = halo(GM, GM, (mx, my), HR, HM, med_send.at[1], med_recv.at[1], True)
     start(gm_halo)
+    gather_b(lambda copy: copy.start())
     pre_halo = halo(VP, VP, (nx, ny), HB, HB, fine_send.at[2], fine_recv.at[2], True)
-    start(pre_halo)
 
     wait_recv(bm_halo)
     MX[0] = 0.5 * (BM[0] + BM[1])
@@ -284,6 +283,7 @@
     gather_r(lambda copy: copy.start())
     pm_halo = halo(PM, PM, (mx, my), HM, HM, med_send.at[2], med_recv.at[2], True)
     start(pm_halo)
+    start(pre_halo)
 
     gather_b(lambda copy: copy.wait_recv())
     crows = ns * cy

time: 42 us -> 41.2 us (0.981)
  Pallas kernels: 37.9 us -> 37 us
    pallas_call x1, Pallas kernels: 37.9 us -> 37 us  [shards(): pl.pallas_call(functools.partial(kernel, nb, ns), out_shape=[jax.ShapeDty...]
where the time goes in v4:
time: 41.2 us; the launch traced here: 40.9 us
  Pallas kernels  37 us (90%)
  local copies, waits for them, and re-layouts  3.3 us (8%)
  between operations  0.65 us (2%)
    pallas_call x1, Pallas kernels, shards(): pl.pallas_call(functools.partial(kernel, nb, ns), out_shape=[jax.ShapeDty...  37 us
    unnamed x6, local copies, waits for them, and re-layouts  3.3 us

profile of v4, /device:TPU:0, one launch (start us, length us, event | category | flops | bytes accessed | tf_op | source)
XLA Modules:
  0.0 40.9 jit_solution(4058067650479688729)
XLA Ops:
  0.6 0.0 copy-start
  0.6 0.9 %copy-done = f32[8,32,256]{2,1,0:T(8,128)S(1)} copy-done((f32[8,32,256]{2,1,0:T(8,128)S(1)}, f32[8,32,256]{2,1,0:T(8,128)}, u32[]{:S(2)}) %copy-start) | copy-done | bytes 262168
  1.6 0.0 copy-start.1
  1.6 0.9 %copy-done.1 = f32[8,32,256]{2,1,0:T(8,128)S(1)} copy-done((f32[8,32,256]{2,1,0:T(8,128)S(1)}, f32[8,32,256]{2,1,0:T(8,128)}, u32[]{:S(2)}) %copy-start.1) | copy-done | bytes 262168
  2.5 37.0 %shard_map.41 = (f32[8,32,256]{2,1,0:T(8,128)S(1)}, f32[8,32,256]{2,1,0:T(8,128)S(1)}) custom-call(f32[8,32,256]{2,1,0:T(8,128)S(1)} %copy-done, f32[8,32,256]{2,1,0:T(8,128)S(1)} %copy-done.1), custom_call_target="tpu_custom_call" | custom-call | tf_op jit(solution)/shard_map/pallas_call | solution.py:413
  39.5 0.7 %copy.6 = f32[8,32,256]{2,1,0:T(8,128)} copy(f32[8,32,256]{2,1,0:T(8,128)S(1)} %get-tuple-element.4) | data formatting | bytes 524288
  40.2 0.7 %copy.7 = f32[8,32,256]{2,1,0:T(8,128)} copy(f32[8,32,256]{2,1,0:T(8,128)S(1)} %get-tuple-element.5) | data formatting | bytes 524288
Async XLA Ops:
  0.6 1.0 %copy-start = (f32[8,32,256]{2,1,0:T(8,128)S(1)}, f32[8,32,256]{2,1,0:T(8,128)}, u32[]{:S(2)}) copy-start(f32[8,32,256]{2,1,0:T(8,128)} %g_in.1) | copy-start | bytes 786436
  1.6 0.9 %copy-start.1 = (f32[8,32,256]{2,1,0:T(8,128)S(1)}, f32[8,32,256]{2,1,0:T(8,128)}, u32[]{:S(2)}) copy-start(f32[8,32,256]{2,1,0:T(8,128)} %b_in.1) | copy-start | bytes 786436
